TPU v7x, 128 devices: a whole 4x4x4 slice. The times are simulated.
128 devices in a mesh: seq: 8 (over x, core), head: 16 (over z, y).
Axes of the slice: x: 4, y: 4, z: 4, core: 2. Of those that a mesh axis runs over, the one named last changes fastest.
Arguments:
- tokens: bfloat16 [1024, 6144], P('seq'), may hold values from -6 to 6
- log_decay: float32 [1024, 32], P('seq', 'head'), may hold values from -1 to 0
- carried_state: float32 [32, 128, 128], P('head'), may hold values from -48 to 48
- q_weight: bfloat16 [6144, 4096], P(None, 'head'), may hold values from -0.078125 to 0.078125
- k_weight: bfloat16 [6144, 4096], P(None, 'head'), may hold values from -0.078125 to 0.078125
- v_weight: bfloat16 [6144, 4096], P(None, 'head'), may hold values from -0.078125 to 0.078125
- out_weight: bfloat16 [4096, 6144], P('head'), may hold values from -0.09375 to 0.09375
- final_gain: bfloat16 [6144], replicated, may hold values from 0.099609375 to 1.8984375
- vocab_weight: bfloat16 [6144, 131072], P(None, ('seq', 'head')), may hold values from -5 to 5
- targets: int32 [1024], replicated, may hold values from 0 to 131071
Outputs:
- loglik: float32 [1024], P('seq')
All inputs are finite; a program needn't handle non-finite values.
Results may differ from a plain program's by a relative error of at most 0.002.
Values may be sent and summed in bfloat16 or wider, within the bound.
No kernel may reach another device: no remote copies, remote signals or barrier semaphores. Data moves between devices by JAX's collectives and lax.ppermute only.
A program may use at most 128 MiB of HBM per device.

v0:
```python
import jax
import jax.numpy as jnp
from jax import lax
from jax.sharding import PartitionSpec as P


def prefix(array, axis, combine, identity):
    length, here = (lax.axis_size(axis), lax.axis_index(axis))
    everything = jax.tree.map(lambda part: lax.all_gather(part, axis), array)
    start = jax.tree.map(
        lambda part, zero: jnp.broadcast_to(jnp.asarray(zero, part.dtype), part.shape),
        array,
        identity,
    )

    def turn(k, before):
        reached = k < here
        new = combine(before, jax.tree.map(lambda part: part[k], everything))
        return jax.tree.map(lambda a, b: jnp.where(reached, a, b), new, before)

    return lax.fori_loop(0, length, turn, start)


def combine_states(earlier, later):
    return (earlier[0] * later[0], later[0][:, None, None] * earlier[1] + later[1])


def shards(
    tokens,
    log_decay,
    carried_state,
    q_weight,
    k_weight,
    v_weight,
    out_weight,
    final_gain,
    vocab_weight,
    targets,
):
    highest = lax.Precision.HIGHEST
    rows_here = tokens.shape[0]
    heads_here = carried_state.shape[0]
    head_size = carried_state.shape[1]
    view = (rows_here, heads_here, head_size)
    queries = (
        jnp.dot(tokens, q_weight, preferred_element_type=jnp.float32)
        .astype(jnp.bfloat16)
        .reshape(view)
    )
    keys_loc = (
        jnp.dot(tokens, k_weight, preferred_element_type=jnp.float32)
        .astype(jnp.bfloat16)
        .reshape(view)
    )
    values = (
        jnp.dot(tokens, v_weight, preferred_element_type=jnp.float32)
        .astype(jnp.bfloat16)
        .reshape(view)
    )
    cumul = jnp.cumsum(log_decay, axis=0)
    last_cum = cumul[-1]
    ends = jnp.exp(last_cum[None, :] - cumul)
    local_state = jnp.einsum(
        "thd,the->hde",
        keys_loc.astype(jnp.float32) * ends[:, :, None],
        values.astype(jnp.float32),
        precision=highest,
    )
    total_decay = jnp.exp(last_cum)
    prefix_decay, prefix_state = prefix(
        (total_decay, local_state),
        "seq",
        combine_states,
        (jnp.ones_like(total_decay), jnp.zeros_like(local_state)),
    )
    lower = jnp.arange(rows_here)[:, None] >= jnp.arange(rows_here)[None, :]
    scores = jnp.einsum("thd,shd->hts", queries, keys_loc, preferred_element_type=jnp.float32)
    diff = jnp.transpose(cumul[:, None, :] - cumul[None, :, :], (2, 0, 1))
    weight = (scores * jnp.exp(jnp.where(lower[None], diff, -1e30))).astype(jnp.bfloat16)
    intra = jnp.einsum("hts,shd->thd", weight, values, preferred_element_type=jnp.float32)
    state_in = prefix_decay[:, None, None] * carried_state + prefix_state
    inter = jnp.exp(cumul)[:, :, None] * jnp.einsum(
        "thd,hde->the", queries.astype(jnp.float32), state_in, precision=highest
    )
    attended = intra + inter
    normed_heads = attended * lax.rsqrt(
        jnp.mean(attended * attended, axis=-1, keepdims=True) + 1e-06
    )
    flat_heads = normed_heads.astype(jnp.bfloat16).reshape(rows_here, heads_here * head_size)
    rows_mine = rows_here // lax.axis_size("head")
    head_index = lax.axis_index("head")
    mixed_all = lax.psum(
        jnp.dot(flat_heads, out_weight, preferred_element_type=jnp.float32), "head"
    )
    mixed = lax.dynamic_slice_in_dim(mixed_all, head_index * rows_mine, rows_mine, 0)
    resid = (
        lax.dynamic_slice_in_dim(tokens, head_index * rows_mine, rows_mine, 0).astype(jnp.float32)
        + mixed
    )
    final_rows = (
        resid
        * lax.rsqrt(jnp.mean(resid * resid, axis=-1, keepdims=True) + 1e-06)
        * final_gain.astype(jnp.float32)
    )
    final_rows = final_rows.astype(jnp.bfloat16)
    vocab_local = vocab_weight.shape[1]
    offset = (lax.axis_index("seq") * lax.axis_size("head") + head_index) * vocab_local
    columns = jnp.arange(vocab_local, dtype=jnp.int32)
    logits = jnp.dot(
        lax.all_gather(final_rows, ("seq", "head"), axis=0, tiled=True),
        vocab_weight,
        preferred_element_type=jnp.float32,
    )
    top = jnp.max(logits, axis=1)
    total = jnp.sum(jnp.exp(logits - top[:, None]), axis=1)
    wanted = targets - offset
    hit = jnp.sum(jnp.where(columns[None, :] == wanted[:, None], logits, 0.0), axis=1)
    top_all = lax.pmax(top, ("seq", "head"))
    total_all, hit_all = lax.psum((total * jnp.exp(top - top_all), hit), ("seq", "head"))
    loglik = hit_all - top_all - jnp.log(total_all)
    return lax.dynamic_slice_in_dim(loglik, lax.axis_index("seq") * rows_here, rows_here, 0)


def solution(mesh):
    return jax.shard_map(
        shards,
        mesh=mesh,
        in_specs=(
            P("seq", None),
            P("seq", "head"),
            P("head", None, None),
            P(None, "head"),
            P(None, "head"),
            P(None, "head"),
            P("head", None),
            P(),
            P(None, ("seq", "head")),
            P(),
        ),
        out_specs=P("seq"),
        check_vma=False,
    )
```

profile of v0, /device:TPU:1, one launch (start us, length us, event | category | flops | bytes accessed | tf_op | source)
XLA Modules:
  0.0 385.3 jit_solution(14718534888018662489)
XLA Ops:
  6.5 0.9 copy.23
  7.5 0.2 reduce_window_sum.11
  7.7 3.0 convolution_convert_fusion
  10.7 0.1 copy.36
  10.8 3.0 fusion.4
  13.8 0.9 fusion.8
  14.7 11.8 %all-gather.1 = f32[8,1,2]{2,1,0:T(1,128)S(1)} all-gather(f32[1,1,2]{2,1,0:T(1,128)S(1)} %get-tuple-element.171), channel_id=1, replica_groups=mesh['seq'=8,'head'=16] {'seq'}, dimensions={0}, use_global_device_ids=true | all-gather | bytes 72 | tf_op jit(solution)/shard_map/all_gather | solution.py:9
  26.6 0.1 copy.24
  26.7 3.1 fusion.5
  29.8 12.0 %all-gather.7.cloned.1.call-done = f32[16,128,128]{2,1,0:T(8,128)} async-done(((f32[2,128,128]{2,1,0:T(8,128)}), f32[16,128,128]{2,1,0:T(8,128)}) %all-gather.7.cloned.1.call-update) | async-done | bytes 1048592 | tf_op jit(solution)/shard_map/all_gather | solution.py:9
  41.8 8.3 %while.16 = (s32[]{:T(128)}, f32[2]{0:T(128)S(1)}, f32[2,128,128]{2,1,0:T(8,128)S(1)}, s32[]{:T(128)}, f32[8,2]{1,0:T(8,128)S(1)}, /*index=5*/f32[8,2,128,128]{3,2,1,0:T(8,128)}, s32[]{:T(128)}, s32[]{:T(128)}) while((s32[]{:T(128)}, f32[2]{0:T(128)S(1)}, f32[2,128,128]{2,1,0:T(8,128)S(1)}, s32[]{:T(128)}, f32[8,2]{1,0:T(8,128)S(1)}, ...), condition=%wide.region_2.3_spmd.clone, body=%wide.region_1.2_spmd.clone.sunk | while | flops 131082 | bytes 393371 | solution.py:21
  41.8 1.0 fusion.48
  42.8 1.0 fusion.48
  43.9 1.0 fusion.48
  44.9 1.0 fusion.48
  46.0 1.0 fusion.48
  47.0 1.0 fusion.48
  48.0 1.0 fusion.48
  49.1 1.0 fusion.48
  50.1 1.9 fusion.1
  52.0 1.2 multiply_reduce_fusion.1
  53.3 2.3 fusion.35
  55.7 0.6 copy-done.1
  56.3 94.3 %all-reduce.3.cloned.1.call-done = f32[128,6144]{1,0:T(8,128)} async-done(((f32[128,6144]{1,0:T(8,128)}), f32[128,6144]{1,0:T(8,128)}) %all-reduce.3.cloned.1.call-update) | async-done | bytes 3145744 | tf_op jit(solution)/shard_map/psum | solution.py:92
  150.6 1.2 multiply_reduce_fusion
  151.8 1.7 multiply_convert_fusion
  153.6 73.3 %all-gather.5.cloned.1.call-done = bf16[1024,6144]{1,0:T(8,128)(2,1)} async-done(((bf16[8,6144]{1,0:T(8,128)(2,1)}), bf16[1024,6144]{1,0:T(8,128)(2,1)}) %all-gather.5.cloned.1.call-update) | async-done | bytes 12582928 | tf_op jit(solution)/shard_map/all_gather | solution.py:110
  226.9 19.4 %fusion.34 = (f32[1024]{0:T(1024)S(1)}, f32[1024,1024]{0,1:T(8,128)}) fusion(bf16[1024,6144]{1,0:T(8,128)(2,1)} %all-gather.5.cloned.1.call-done, bf16[6144,1024]{1,0:T(8,128)(2,1)} %param.20), kind=kOutput, calls=%fused_computation.57 | convolution fusion | flops 12885949440 | bytes 29364224 | tf_op jit(solution)/shard_map/dot_general | solution.py:109
  246.3 64.4 %pmax.7 = f32[1024]{0:T(1024)S(1)} all-reduce(f32[1024]{0:T(1024)S(1)} %get-tuple-element.174), channel_id=1, replica_groups=mesh['seq'=8,'head'=16] {'seq','head'}, use_global_device_ids=true, to_apply=%region_9.10 | all-reduce | flops 1024 | bytes 8192 | tf_op jit(solution)/shard_map/pmax | solution.py:118
  310.7 3.3 select_reduce_fusion
  314.0 64.2 %all-reduce = (f32[1024]{0:T(1024)S(1)}, f32[1024]{0:T(1024)S(1)}) all-reduce(f32[1024]{0:T(1024)S(1)} %exponential_multiply_fusion, f32[1024]{0:T(1024)S(1)} %get-tuple-element.150), channel_id=1, replica_groups=mesh['seq'=8,'head'=16] {'seq','head'}, use_global_device_ids=true, to_apply=%region_11.12 | all-reduce | flops 2048 | bytes 16384 | tf_op jit(solution)/shard_map/psum | solution.py:119
  378.2 0.6 dynamic_slice.25
  (33 shorter events, 0.5 us)
Async XLA Ops:
  6.5 46.7 %copy-start = (bf16[256,6144]{1,0:T(8,128)(2,1)S(1)}, bf16[256,6144]{1,0:T(8,128)(2,1)}, u32[]{:S(2)}) copy-start(bf16[256,6144]{1,0:T(8,128)(2,1)} %param.18) | copy-start | bytes 9437188
  6.5 35.2 %all-gather.7.cloned.1.call-start = ((), (), s32[]{:S(2)}) async-start(), calls=%async_computation.2 | async-start | bytes 1179648 | tf_op jit(solution)/shard_map/all_gather | solution.py:9
  14.7 135.9 %all-reduce.3.cloned.1.call-start = ((), (), s32[]{:S(2)}) async-start(), calls=%async_computation | async-start | bytes 6291456 | tf_op jit(solution)/shard_map/psum | solution.py:92
  55.6 0.7 copy-start.1
  55.6 98.0 %copy-start.2 = (s32[1024]{0:T(1024)S(1)}, s32[1024]{0:T(1024)}, u32[]{:S(2)}) copy-start(s32[1024]{0:T(1024)} %param.21) | copy-start | bytes 12292
  55.6 171.3 %all-gather.5.cloned.1.call-start = ((), (), s32[]{:S(2)}) async-start(), calls=%async_computation.1 | async-start | bytes 12681216 | tf_op jit(solution)/shard_map/all_gather | solution.py:110
Sparse Core Ops, SparseCore 0:
  14.8 26.9 all-gather.6
  55.7 94.8 all-reduce.2
  153.7 73.0 all-gather.4
where the time goes:
time: 386 us; the launch traced here: 385 us
  waiting for transfers between devices  180 us (47%)
  blocking collectives  140 us (36%)
  matrix products  34.7 us (9%)
  other arithmetic  14.5 us (4%)
  between operations  13.2 us (3%)
    psum x1, waiting for transfers between devices, shards(): lax.psum(jnp.dot(flat_heads, out_weight, preferred_element_type=jnp.float...  94.3 us
    all_gather x1, waiting for transfers between devices, shards(): lax.all_gather(final_rows, ('seq', 'head'), axis=0, tiled=True)  73.3 us
    pmax x1, blocking collectives, shards(): top_all = lax.pmax(top, ('seq', 'head'))  64.4 us
    psum x1, blocking collectives, shards(): lax.psum((total * jnp.exp(top - top_all), hit), ('seq', 'head'))  64.2 us
    dot_general x1, matrix products, shards(): jnp.dot(lax.all_gather(final_rows, ('seq', 'head'), axis=0, tiled=True),...  19.4 us
    all_gather x1, waiting for transfers between devices, prefix(): everything = jax.tree.map(lambda part: lax.all_gather(part, axis), array)  12 us
    all_gather x1, blocking collectives, prefix(): everything = jax.tree.map(lambda part: lax.all_gather(part, axis), array)  11.8 us
    select_n x16, other arithmetic, turn(): return jax.tree.map(lambda a, b: jnp.where(reached, a, b), new, before)  8.09 us
  transfers between devices with their start and end apart: 3, of which 3 were waited for; matrix products, arithmetic and copies ran while one was open for 1% of the time, Pallas kernels for 0%

commit v1 on v0

--- a/solution.py
+++ b/solution.py
@@ -116,7 +116,7 @@
     wanted = targets - offset
     hit = jnp.sum(jnp.where(columns[None, :] == wanted[:, None], logits, 0.0), axis=1)
     top_all = lax.pmax(top, ("seq", "head"))
-    total_all, hit_all = lax.psum((total * jnp.exp(top - top_all), hit), ("seq", "head"))
+    total_all, hit_all = lax.psum(lax.psum((total * jnp.exp(top - top_all), hit), "head"), "seq")
     loglik = hit_all - top_all - jnp.log(total_all)
     return lax.dynamic_slice_in_dim(loglik, lax.axis_index("seq") * rows_here, rows_here, 0)
 

time: 386 us -> 373 us (0.966)
  blocking collectives: 140 us -> 128 us
    psum x1 -> x2, blocking collectives: 64.2 us -> 51.3 us  [the longest x1 31.3 us: shards(): lax.psum((total * jnp.exp(top - top_all), hit), 'head')]
where the time goes in v1:
time: 373 us; the launch traced here: 372 us
  waiting for transfers between devices  180 us (48%)
  blocking collectives  128 us (34%)
  matrix products  34.7 us (9%)
  other arithmetic  14.5 us (4%)
  between operations  13.3 us (4%)
    psum x1, waiting for transfers between devices, shards(): lax.psum(jnp.dot(flat_heads, out_weight, preferred_element_type=jnp.float...  94.3 us
    all_gather x1, waiting for transfers between devices, shards(): lax.all_gather(final_rows, ('seq', 'head'), axis=0, tiled=True)  73.3 us
    pmax x1, blocking collectives, shards(): top_all = lax.pmax(top, ('seq', 'head'))  64.4 us
    psum x1, blocking collectives, shards(): lax.psum((total * jnp.exp(top - top_all), hit), 'head')  31.3 us
    psum x1, blocking collectives, shards(): lax.psum(lax.psum((total * jnp.exp(top - top_all), hit), 'head'), 'seq')  20 us
    dot_general x1, matrix products, shards(): jnp.dot(lax.all_gather(final_rows, ('seq', 'head'), axis=0, tiled=True),...  19.4 us
    all_gather x1, waiting for transfers between devices, prefix(): everything = jax.tree.map(lambda part: lax.all_gather(part, axis), array)  12 us
    all_gather x1, blocking collectives, prefix(): everything = jax.tree.map(lambda part: lax.all_gather(part, axis), array)  11.8 us
  transfers between devices with their start and end apart: 3, of which 3 were waited for; matrix products, arithmetic and copies ran while one was open for 1% of the time, Pallas kernels for 0%

profile of v1, /device:TPU:1, one launch (start us, length us, event | category | flops | bytes accessed | tf_op | source)
XLA Modules:
  0.0 372.4 jit_solution(12365409129073786822)
XLA Ops:
  6.5 0.9 copy.23
  7.5 0.2 reduce_window_sum.11
  7.7 3.0 convolution_convert_fusion
  10.7 0.1 copy.36
  10.8 3.0 fusion.4
  13.8 0.9 fusion.8
  14.7 11.8 %all-gather.1 = f32[8,1,2]{2,1,0:T(1,128)S(1)} all-gather(f32[1,1,2]{2,1,0:T(1,128)S(1)} %get-tuple-element.173), channel_id=1, replica_groups=mesh['seq'=8,'head'=16] {'seq'}, dimensions={0}, use_global_device_ids=true | all-gather | bytes 72 | tf_op jit(solution)/shard_map/all_gather | solution.py:9
  26.7 3.1 fusion.5
  29.8 12.0 %all-gather.7.cloned.1.call-done = f32[16,128,128]{2,1,0:T(8,128)} async-done(((f32[2,128,128]{2,1,0:T(8,128)}), f32[16,128,128]{2,1,0:T(8,128)}) %all-gather.7.cloned.1.call-update) | async-done | bytes 1048592 | tf_op jit(solution)/shard_map/all_gather | solution.py:9
  41.8 8.3 %while.16 = (s32[]{:T(128)}, f32[2]{0:T(128)S(1)}, f32[2,128,128]{2,1,0:T(8,128)S(1)}, s32[]{:T(128)}, f32[8,2]{1,0:T(8,128)S(1)}, /*index=5*/f32[8,2,128,128]{3,2,1,0:T(8,128)}, s32[]{:T(128)}, s32[]{:T(128)}) while((s32[]{:T(128)}, f32[2]{0:T(128)S(1)}, f32[2,128,128]{2,1,0:T(8,128)S(1)}, s32[]{:T(128)}, f32[8,2]{1,0:T(8,128)S(1)}, ...), condition=%wide.region_2.3_spmd.clone, body=%wide.region_1.2_spmd.clone.sunk | while | flops 131082 | bytes 393371 | solution.py:21
  41.8 1.0 fusion.48
  42.8 1.0 fusion.48
  43.9 1.0 fusion.48
  44.9 1.0 fusion.48
  46.0 1.0 fusion.48
  47.0 1.0 fusion.48
  48.0 1.0 fusion.48
  49.1 1.0 fusion.48
  50.1 1.9 fusion.1
  52.0 1.2 multiply_reduce_fusion.1
  53.3 2.3 fusion.35
  55.7 0.6 copy-done.1
  56.3 94.3 %all-reduce.4.cloned.1.call-done = f32[128,6144]{1,0:T(8,128)} async-done(((f32[128,6144]{1,0:T(8,128)}), f32[128,6144]{1,0:T(8,128)}) %all-reduce.4.cloned.1.call-update) | async-done | bytes 3145744 | tf_op jit(solution)/shard_map/psum | solution.py:92
  150.6 1.2 multiply_reduce_fusion
  151.8 1.7 multiply_convert_fusion
  153.6 73.3 %all-gather.5.cloned.1.call-done = bf16[1024,6144]{1,0:T(8,128)(2,1)} async-done(((bf16[8,6144]{1,0:T(8,128)(2,1)}), bf16[1024,6144]{1,0:T(8,128)(2,1)}) %all-gather.5.cloned.1.call-update) | async-done | bytes 12582928 | tf_op jit(solution)/shard_map/all_gather | solution.py:110
  226.9 19.4 %fusion.34 = (f32[1024]{0:T(1024)S(1)}, f32[1024,1024]{0,1:T(8,128)}) fusion(bf16[1024,6144]{1,0:T(8,128)(2,1)} %all-gather.5.cloned.1.call-done, bf16[6144,1024]{1,0:T(8,128)(2,1)} %param.20), kind=kOutput, calls=%fused_computation.57 | convolution fusion | flops 12885949440 | bytes 29364224 | tf_op jit(solution)/shard_map/dot_general | solution.py:109
  246.3 64.4 %pmax.7 = f32[1024]{0:T(1024)S(1)} all-reduce(f32[1024]{0:T(1024)S(1)} %get-tuple-element.176), channel_id=1, replica_groups=mesh['seq'=8,'head'=16] {'seq','head'}, use_global_device_ids=true, to_apply=%region_10.11 | all-reduce | flops 1024 | bytes 8192 | tf_op jit(solution)/shard_map/pmax | solution.py:118
  310.7 3.3 select_reduce_fusion
  314.0 31.3 %all-reduce = (f32[1024]{0:T(1024)S(1)}, f32[1024]{0:T(1024)S(1)}) all-reduce(f32[1024]{0:T(1024)S(1)} %exponential_multiply_fusion, f32[1024]{0:T(1024)S(1)} %get-tuple-element.150), channel_id=1, replica_groups=mesh['seq'=8,'head'=16] {'head'}, use_global_device_ids=true, to_apply=%region_12.13 | all-reduce | flops 2048 | bytes 16384 | tf_op jit(solution)/shard_map/psum | solution.py:119
  345.3 20.0 %all-reduce.1 = (f32[1024]{0:T(1024)S(1)}, f32[1024]{0:T(1024)S(1)}) all-reduce(f32[1024]{0:T(1024)S(1)} %get-tuple-element.164, f32[1024]{0:T(1024)S(1)} %get-tuple-element.165), channel_id=1, replica_groups=mesh['seq'=8,'head'=16] {'seq'}, use_global_device_ids=true, to_apply=%region_13.14 | all-reduce | flops 2048 | bytes 16384 | tf_op jit(solution)/shard_map/psum | solution.py:119
  365.3 0.6 dynamic_slice.25
  (34 shorter events, 0.6 us)
Async XLA Ops:
  6.5 46.7 %copy-start = (bf16[256,6144]{1,0:T(8,128)(2,1)S(1)}, bf16[256,6144]{1,0:T(8,128)(2,1)}, u32[]{:S(2)}) copy-start(bf16[256,6144]{1,0:T(8,128)(2,1)} %param.18) | copy-start | bytes 9437188
  6.5 35.2 %all-gather.7.cloned.1.call-start = ((), (), s32[]{:S(2)}) async-start(), calls=%async_computation.2 | async-start | bytes 1179648 | tf_op jit(solution)/shard_map/all_gather | solution.py:9
  14.7 135.9 %all-reduce.4.cloned.1.call-start = ((), (), s32[]{:S(2)}) async-start(), calls=%async_computation | async-start | bytes 6291456 | tf_op jit(solution)/shard_map/psum | solution.py:92
  55.6 0.7 copy-start.1
  55.6 98.0 %copy-start.2 = (s32[1024]{0:T(1024)S(1)}, s32[1024]{0:T(1024)}, u32[]{:S(2)}) copy-start(s32[1024]{0:T(1024)} %param.21) | copy-start | bytes 12292
  55.6 171.3 %all-gather.5.cloned.1.call-start = ((), (), s32[]{:S(2)}) async-start(), calls=%async_computation.1 | async-start | bytes 12681216 | tf_op jit(solution)/shard_map/all_gather | solution.py:110
Sparse Core Ops, SparseCore 0:
  14.8 26.9 all-gather.6
  55.7 94.8 all-reduce.3
  153.7 73.0 all-gather.4
